TPU v7x, 256 devices: a whole 4x4x8 slice. The times are simulated.
256 devices in a mesh: dp: 32 (over z, x), sub: 8 (over y, core).
Axes of the slice: x: 4, y: 4, z: 8, core: 2. Of those that a mesh axis runs over, the one named last changes fastest.
Arguments:
- tokens: bfloat16 [131072, 1024], P(('dp', 'sub')), may hold values from -6 to 6
- lengths: int32 [32, 8, 4], P('dp', 'sub'), may hold values from 1 to 341, 512 in all within a row
- w_up: bfloat16 [4096, 1024], P('dp'), may hold values from -0.1875 to 0.1875
- up_bias: bfloat16 [4096], P('dp'), may hold values from -3 to 3
- w_down: bfloat16 [4096, 1024], P('dp'), may hold values from -0.09375 to 0.09375
- down_bias: float32 [1024], replicated, may hold values from -3 to 3
- ln_gain: float32 [1024], replicated, may hold values from 0.5 to 1.5
- ln_bias: float32 [1024], replicated, may hold values from -0.6 to 0.6
- stored: bfloat16 [65536, 1024], P('dp', 'sub'), may hold values from -6 to 6
- stored_codes: int32 [8, 65536], P('sub', 'dp'), may hold values from 0 to 4095
- new_codes: int32 [8, 1024], P('sub'), may hold values from 0 to 4095
- centroids: float32 [8, 4096, 128], P('sub'), may hold values from -6 to 6
Outputs:
- embeds: bfloat16 [1024, 1024], P('dp', 'sub')
- updated: float32 [8, 4096, 128], P('sub')
Inputs may be any that keep to these rules, and one draw needn't show every extreme that they name: The 4 lengths of one block sum to 512; in every block the longest is exactly 341.
All inputs are finite; a program needn't handle non-finite values.
Results may differ from a plain program's by a relative error of at most 0.015.
Values may be sent and summed in bfloat16 or wider, within the bound.
A program may use at most 128 MiB of HBM per device.

v0:
```python
import jax
import jax.numpy as jnp
from jax import lax
from jax.sharding import PartitionSpec as P


def complete_layer(tokens, ffn_total, lengths, down_bias, ln_gain, ln_bias):
    resid = tokens.astype(jnp.float32) + ffn_total + down_bias
    center = resid - jnp.mean(resid, axis=-1, keepdims=True)
    spread = jnp.mean(center * center, axis=-1, keepdims=True)
    layer_out = (center * lax.rsqrt(spread + 1e-12) * ln_gain + ln_bias).astype(jnp.bfloat16)
    passage_len = lengths.reshape(-1)
    ending = jnp.cumsum(passage_len, dtype=jnp.int32)
    opening = ending - passage_len
    places = jnp.arange(tokens.shape[0], dtype=jnp.int32)
    member = ((places[None, :] >= opening[:, None]) & (places[None, :] < ending[:, None])).astype(
        jnp.bfloat16
    )
    pooled = jnp.dot(member, layer_out, preferred_element_type=jnp.float32) / passage_len[
        :, None
    ].astype(jnp.float32)
    scaling = lax.rsqrt(jnp.mean(pooled * pooled, axis=-1, keepdims=True) + 1e-06)
    return (pooled * scaling).astype(jnp.bfloat16)


def code_tallies(vectors, codes, code_count, sub_width):
    subspaces = codes.shape[0]
    row_count = vectors.shape[0]
    grouped_vectors = vectors.reshape(row_count, subspaces, sub_width)
    width_codes = min(512, code_count)

    def one_group(group_index):
        labels = group_index * width_codes + jnp.arange(width_codes, dtype=jnp.int32)
        assignment_matrix = (codes[:, None, :] == labels[None, :, None]).astype(jnp.bfloat16)
        centroid_totals = jnp.einsum(
            "ybg,gyv->ybv", assignment_matrix, grouped_vectors, preferred_element_type=jnp.float32
        )
        counts = jnp.sum(assignment_matrix, axis=2, dtype=jnp.float32)
        return (centroid_totals, counts)

    centroid_totals, counts = lax.map(
        one_group, jnp.arange(code_count // width_codes, dtype=jnp.int32)
    )
    centroid_totals = jnp.moveaxis(centroid_totals, 0, 1).reshape(subspaces, code_count, sub_width)
    counts = jnp.moveaxis(counts, 0, 1).reshape(subspaces, code_count)
    return (centroid_totals, counts)


def on_device(
    tokens,
    lengths,
    w_up,
    up_bias,
    w_down,
    down_bias,
    ln_gain,
    ln_bias,
    stored,
    stored_codes,
    new_codes,
    centroids,
):
    code_count = centroids.shape[1]
    sub_width = centroids.shape[2]
    up_rows = lax.all_gather(w_up, "dp", axis=0, tiled=True)
    bias_matrix_rows = lax.all_gather(up_bias, "dp", axis=0, tiled=True)
    down_rows = lax.all_gather(w_down, "dp", axis=0, tiled=True)
    preact = lax.dot_general(
        tokens, up_rows, (((1,), (1,)), ((), ())), preferred_element_type=jnp.float32
    )
    hidden = jax.nn.gelu(preact + bias_matrix_rows.astype(jnp.float32), approximate=False).astype(
        jnp.bfloat16
    )
    ffn_total = jnp.dot(hidden, down_rows, preferred_element_type=jnp.float32)
    embedded = complete_layer(tokens, ffn_total, lengths, down_bias, ln_gain, ln_bias)
    incoming_rows = lax.all_to_all(embedded, "sub", split_axis=1, concat_axis=0, tiled=True)
    group_rows = incoming_rows.shape[0]
    own_codes = lax.dynamic_slice_in_dim(
        new_codes, lax.axis_index("dp") * group_rows, group_rows, 1
    )
    vectors = jnp.concatenate([stored, incoming_rows], axis=0)
    codes = jnp.concatenate([stored_codes, own_codes], axis=1)
    centroid_totals, counts = code_tallies(vectors, codes, code_count, sub_width)
    centroid_totals, counts = (
        lax.psum(centroid_totals.astype(jnp.bfloat16), "dp").astype(jnp.float32),
        lax.psum(counts.astype(jnp.bfloat16), "dp").astype(jnp.float32),
    )
    updated = (centroid_totals + centroids) / (counts[:, :, None] + 1.0)
    return (incoming_rows, updated)


def solution(mesh):
    return jax.shard_map(
        on_device,
        mesh=mesh,
        in_specs=(
            P(("dp", "sub"), None),
            P("dp", "sub", None),
            P("dp", None),
            P("dp"),
            P("dp", None),
            P(),
            P(),
            P(),
            P("dp", "sub"),
            P("sub", "dp"),
            P("sub", None),
            P("sub", None, None),
        ),
        out_specs=(P("dp", "sub"), P("sub", None, None)),
        check_vma=False,
    )
```

profile of v0, /device:TPU:1, one launch (start us, length us, event | category | flops | bytes accessed | tf_op | source)
XLA Modules:
  0.0 436.9 jit_solution(12522110468562468235)
XLA Ops:
  7.2 0.0 all-gather.4.cloned.1.call-start
  7.2 0.7 all-gather.4.cloned.1.call-update
  7.9 0.0 all-gather.6.cloned.1.call-start
  8.0 0.7 all-gather.6.cloned.1.call-update
  8.7 35.5 %all-gather = bf16[32,1,128]{2,1,0:T(2,128)(2,1)S(1)} all-gather(bf16[1,1,128]{2,1,0:T(2,128)(2,1)} %bitcast.45), channel_id=1, replica_groups=mesh['dp'=32,'sub'=8] {'dp'}, dimensions={0}, use_global_device_ids=true | all-gather | bytes 8448 | tf_op jit(solution)/shard_map/all_gather | solution.py:66
  44.2 0.8 reduce-window.7
  45.0 0.1 constant_dynamic-slice_fusion
  45.1 0.7 bitcast_convert_fusion
  45.7 0.7 bitcast_subtract_fusion
  46.4 66.1 %all-gather.4.cloned.1.call-done = bf16[4096,1024]{1,0:T(8,128)(2,1)} async-done(((bf16[128,1024]{1,0:T(8,128)(2,1)}), bf16[4096,1024]{1,0:T(8,128)(2,1)}) %all-gather.4.cloned.1.call-update) | async-done | bytes 8388624 | tf_op jit(solution)/shard_map/all_gather | solution.py:65
  112.5 98.0 %all-gather.6.cloned.1.call-done = bf16[4096,1024]{1,0:T(8,128)(2,1)} async-done(((bf16[128,1024]{1,0:T(8,128)(2,1)}), bf16[4096,1024]{1,0:T(8,128)(2,1)}) %all-gather.6.cloned.1.call-update) | async-done | bytes 8388624 | tf_op jit(solution)/shard_map/all_gather | solution.py:67
  210.6 30.8 %fusion.91 = (f32[512]{0:T(512)S(1)}, f32[512,1024]{1,0:T(8,128)S(1)}) fusion(f32[1024]{0:T(1024)} %param.19, bf16[4096,1024]{1,0:T(8,128)(2,1)} %all-gather.6.cloned.1.call-done, bf16[512,1024]{1,0:T(8,128)(2,1)} %param.14, bf16[4096,1024]{1,0:T(8,128)(2,1)} %all-gather.4.cloned.1.call-done, f32[4096]{0:T(1024)S(1)} %bitcast.43), kind=kOutput, calls=%fused_computation.117 | convolution fusion | flops 8730443776 | bytes 19945472 | tf_op jit(solution)/shard_map/dot_general | solution.py:74
  241.4 0.3 multiply_reduce_fusion
  241.8 0.9 copy-done.2
  242.7 2.6 multiply_reduce_fusion.1
  245.3 0.7 fusion.56
  246.0 5.4 %all-to-all-start = ((bf16[4,8,128]{2,0,1:T(4,128)(2,1)}), bf16[4,8,128]{2,0,1:T(4,128)(2,1)S(1)}, u32[]{:S(2)}, u32[]{:S(2)}) async-start(bf16[4,8,128]{2,0,1:T(4,128)(2,1)} %fusion.56), calls=%async_computation | async-start | bytes 16384 | tf_op jit(solution)/shard_map/all_to_all | solution.py:76
  251.4 4.6 %all-to-all-done = bf16[4,8,128]{2,0,1:T(4,128)(2,1)S(1)} async-done(((bf16[4,8,128]{2,0,1:T(4,128)(2,1)}), bf16[4,8,128]{2,0,1:T(4,128)(2,1)S(1)}, u32[]{:S(2)}, u32[]{:S(2)}) %all-to-all-start) | async-done | bytes 8224 | tf_op jit(solution)/shard_map/all_to_all | solution.py:76
  256.0 30.1 %while.12 = (s32[]{:T(128)}, bf16[8,1,512,128]{3,2,1,0:T(8,128)(2,1)}, bf16[8,1,512]{2,1,0:T(2,128)(2,1)S(1)}, s32[1,2080]{1,0:T(1,128)S(1)}, s32[8]{0:T(128)S(1...) while((s32[]{:T(128)}, bf16[8,1,512,128]{3,2,1,0:T(8,128)(2,1)}, ...), condition=%wide.region_6.7_spmd, body=%wide.region_4.6_spmd.sunk | while | flops 277954560 | bytes 840833 | solution.py:41
  256.0 0.6 dynamic_slice.10
  257.3 1.5 fusion.100
  258.8 1.0 convert_reduce_fusion.2
  259.8 0.6 dynamic_slice.10
  261.1 1.5 fusion.100
  262.5 1.0 convert_reduce_fusion.2
  263.5 0.6 dynamic_slice.10
  264.8 1.5 fusion.100
  266.3 1.0 convert_reduce_fusion.2
  267.3 0.6 dynamic_slice.10
  268.6 1.5 fusion.100
  270.0 1.0 convert_reduce_fusion.2
  271.0 0.6 dynamic_slice.10
  272.3 1.5 fusion.100
  273.8 1.0 convert_reduce_fusion.2
  274.8 0.6 dynamic_slice.10
  276.1 1.5 fusion.100
  277.6 1.0 convert_reduce_fusion.2
  278.6 0.6 dynamic_slice.10
  279.8 1.5 fusion.100
  281.3 1.0 convert_reduce_fusion.2
  282.3 0.6 dynamic_slice.10
  283.6 1.5 fusion.100
  285.1 1.0 convert_reduce_fusion.2
  286.1 0.0 all-reduce.2.cloned.1.call-update
  286.1 111.8 %psum.15 = bf16[1,4096]{1,0:T(2,128)(2,1)S(1)} all-reduce(bf16[1,4096]{1,0:T(2,128)(2,1)S(1)} %bitcast.44), channel_id=1, replica_groups=mesh['dp'=32,'sub'=8] {'dp'}, use_global_device_ids=true, to_apply=%region_8.9 | all-reduce | flops 4096 | bytes 16384 | tf_op jit(solution)/shard_map/psum | solution.py:86
  397.9 29.1 %all-reduce.2.cloned.1.call-done = bf16[1,4096,128]{2,1,0:T(8,128)(2,1)} async-done(((bf16[1,4096,128]{2,1,0:T(8,128)(2,1)}), bf16[1,4096,128]{2,1,0:T(8,128)(2,1)}) %all-reduce.2.cloned.1.call-update) | async-done | bytes 1048592 | tf_op jit(solution)/shard_map/psum | solution.py:85
  427.0 2.7 add_divide_fusion
  429.7 0.6 copy.31
  (48 shorter events, 0.5 us)
Async XLA Ops:
  7.2 37.8 %copy-start = (s32[1,1024]{1,0:T(1,128)S(1)}, s32[1,1024]{1,0:T(1,128)}, u32[]{:S(2)}) copy-start(s32[1,1024]{1,0:T(1,128)} %param.24) | copy-start | bytes 12292
  7.2 105.4 %all-gather.4.cloned.1.call-start = ((), (), s32[]{:S(2)}) async-start(), calls=%async_computation.1 | async-start | bytes 8650752 | tf_op jit(solution)/shard_map/all_gather | solution.py:65
  7.9 202.7 %all-gather.6.cloned.1.call-start = ((), (), s32[]{:S(2)}) async-start(), calls=%async_computation.2 | async-start | bytes 8650752 | tf_op jit(solution)/shard_map/all_gather | solution.py:67
  210.6 32.1 %copy-start.5 = (f32[1024]{0:T(1024)S(1)}, f32[1024]{0:T(1024)}, u32[]{:S(2)}) copy-start(f32[1024]{0:T(1024)} %param.21) | copy-start | bytes 12292
  210.6 32.1 %copy-start.6 = (f32[1024]{0:T(1024)S(1)}, f32[1024]{0:T(1024)}, u32[]{:S(2)}) copy-start(f32[1024]{0:T(1024)} %param.20) | copy-start | bytes 12292
  210.6 40.8 %copy-start.4 = (s32[1,2048]{1,0:T(1,128)S(1)}, s32[1,2048]{1,0:T(1,128)}, u32[]{:S(2)}) copy-start(s32[1,2048]{1,0:T(1,128)} %param.23) | copy-start | bytes 24580
  210.6 45.4 %copy-start.3 = (bf16[2048,128]{1,0:T(8,128)(2,1)S(1)}, bf16[2048,128]{1,0:T(8,128)(2,1)}, u32[]{:S(2)}) copy-start(bf16[2048,128]{1,0:T(8,128)(2,1)} %param.22) | copy-start | bytes 1572868
  241.4 1.3 copy-start.2
  242.7 184.3 %copy-start.1 = (f32[1,4096,128]{2,1,0:T(8,128)S(1)}, f32[1,4096,128]{2,1,0:T(8,128)}, u32[]{:S(2)}) copy-start(f32[1,4096,128]{2,1,0:T(8,128)} %param.25) | copy-start | bytes 6291460
  246.0 10.0 %all-to-all-start = ((bf16[4,8,128]{2,0,1:T(4,128)(2,1)}), bf16[4,8,128]{2,0,1:T(4,128)(2,1)S(1)}, u32[]{:S(2)}, u32[]{:S(2)}) async-start(bf16[4,8,128]{2,0,1:T(4,128)(2,1)} %fusion.56), calls=%async_computation | async-start | bytes 16384 | tf_op jit(solution)/shard_map/all_to_all | solution.py:76
  251.3 175.7 %all-reduce.2.cloned.1.call-start = ((), (), s32[]{:S(2)}) async-start(), calls=%async_computation.3 | async-start | bytes 2097152 | tf_op jit(solution)/shard_map/psum | solution.py:85
Sparse Core Ops, SparseCore 0:
  10.6 101.8 all-gather.3
  115.1 95.4 all-gather.5
  286.2 140.7 all-reduce.1
where the time goes:
time: 441 us; the launch traced here: 437 us
  waiting for transfers between devices  199 us (45%)
  blocking collectives  147 us (33%)
  matrix products  45.1 us (10%)
  other arithmetic  14 us (3%)
  between operations  13.8 us (3%)
  local copies, waits for them, and re-layouts  6.44 us (1%)
  loops' own time  5.45 us (1%)
  starting transfers between devices  5.43 us (1%)
    psum x1, blocking collectives, on_device(): lax.psum(counts.astype(jnp.bfloat16), 'dp').astype(jnp.float32)  112 us
    all_gather x1, waiting for transfers between devices, on_device(): down_rows = lax.all_gather(w_down, 'dp', axis=0, tiled=True)  98 us
    all_gather x1, waiting for transfers between devices, on_device(): up_rows = lax.all_gather(w_up, 'dp', axis=0, tiled=True)  66.1 us
    all_gather x1, blocking collectives, on_device(): bias_matrix_rows = lax.all_gather(up_bias, 'dp', axis=0, tiled=True)  35.5 us
    dot_general x1, matrix products, on_device(): ffn_total = jnp.dot(hidden, down_rows, preferred_element_type=jnp.float32)  30.8 us
    psum x1, waiting for transfers between devices, on_device(): lax.psum(centroid_totals.astype(jnp.bfloat16), 'dp').astype(jnp.float32)  29.1 us
    dot_general x8, matrix products, one_group(): jnp.einsum('ybg,gyv->ybv', assignment_matrix, grouped_vectors, preferred_...  11.8 us
  transfers between devices with their start and end apart: 4, of which 4 were waited for; matrix products, arithmetic and copies ran while one was open for 1% of the time, Pallas kernels for 0%

commit v1 on v0

v1 whole, which is shorter than its diff:
```python
import functools

import jax
import jax.numpy as jnp
from jax import lax
from jax.experimental import pallas as pl
from jax.experimental.pallas import tpu as pltpu
from jax.sharding import PartitionSpec as P

MESH = pl.DeviceIdType.MESH
NX, NZ, NS = 4, 8, 8
BF, F32 = jnp.bfloat16, jnp.float32

GELU_P = (
    0.7978849411010742,
    0.03633308410644531,
    -3.259497316321358e-05,
    -5.530619455385022e-05,
    3.964744792028796e-06,
    -1.322633664813111e-07,
    1.7561715415226331e-09,
)
GELU_CAP = 30.0

SLOT_UP = (0, 1, 3, 5, 7)
SLOT_DOWN = (0, 2, 4, 6, 7)


def gelu(p):
    t = jnp.minimum(p * p, GELU_CAP)
    q = jnp.full_like(t, GELU_P[-1])
    for coefficient in GELU_P[-2::-1]:
        q = q * t + coefficient
    half = 0.5 * p
    return half + half * jnp.tanh(p * q)


def tidy_block(total):
    n = total.shape[0]
    count = 256.0 * total[:, 128:129, :] + total[:, 129:130, :]
    return jnp.concatenate([total[:, :128, :], count_rows(count, n)], axis=1).astype(BF)


def count_rows(count, n):
    high = jnp.floor(count * (1.0 / 256.0))
    low = count - 256.0 * high
    row = lax.broadcasted_iota(jnp.int32, (n, 16, 128), 1)
    return jnp.where(row == 0, high, jnp.where(row == 1, low, 0.0))


def layer_kernel(
    tokens, w_up, w_down, stored, lengths, up_bias, down_bias, ln_gain, ln_bias, codes,
    e_out, f_out,
    x_buf, gu, gd, acc, ps, pr, sv, tt, ra, rb, rc, ff, bb, em, er, ee, pooled,
    send_sem, recv_sem, local_sem,
):
    dp, s = lax.axis_index("dp"), lax.axis_index("sub")
    z, x, core = dp // NX, dp % NX, s % 2
    quarter = ((s // 2) % 2) * 2 + core

    def z_peer(k):
        return (((z + k + NZ) % NZ) * NX + x, s)

    def x_peer(k):
        return (z * NX + (x + k + NX) % NX, s)

    def s_peer(k):
        return (dp, (s + k) % NS)

    mate = (dp, s + 1 - 2 * core)
    partner = (dp, (s + 2 * core - 1 + NS) % NS)

    used = [0, 0]
    started = []

    def remote(src, dst, device):
        i = used[0]
        used[0] += 1
        copy = pltpu.make_async_remote_copy(
            src_ref=src, dst_ref=dst, send_sem=send_sem.at[i], recv_sem=recv_sem.at[i],
            device_id=device, device_id_type=MESH,
        )
        started.append(copy)
        return copy

    def local(src, dst):
        i = used[1]
        used[1] += 1
        copy = pltpu.make_async_copy(src, dst, local_sem.at[i])
        copy.start()
        return copy

    row0 = pl.multiple_of(quarter * 32, 32)
    load_up = local(w_up.at[pl.ds(row0, 32)], gu.at[0, 0, 0])
    load_down = local(w_down.at[pl.ds(row0, 32)], gd.at[0, 0, 0])
    load_x = local(tokens, x_buf.at[0])
    load_s = local(stored, sv.at[:, pl.ds(0, 128)])

    barrier = pltpu.get_barrier_semaphore()
    peers = [z_peer(k) for k in range(1, NZ)] + [x_peer(k) for k in range(1, NX)] + [s_peer(k) for k in range(1, NS)]
    for device in peers:
        pl.semaphore_signal(barrier, inc=1, device_id=device, device_id_type=MESH)

    lane = lax.broadcasted_iota(jnp.int32, (8, 128), 1)
    own_bias = jnp.where(lane // 32 == quarter, jnp.broadcast_to(up_bias[...].astype(F32), (8, 128)), 0.0)
    own_bias = own_bias + pltpu.roll(own_bias, 64, 1)
    bb[0, 0] = own_bias + pltpu.roll(own_bias, 32, 1)
    sv[:, 128:256] = jnp.ones((2048, 128), BF)

    load_up.wait()
    load_down.wait()
    load_x.wait()
    pl.semaphore_wait(barrier, len(peers))

    flows = {}
    buffers = {"u": gu, "d": gd}

    def piece(kind, jx, slot, half):
        ref = buffers[kind].at[slot // 4, jx, slot % 4]
        return ref if half is None else ref.at[pl.ds(16 * half, 16)]

    def send(kind, axis, direction, src, dst, half):
        device = z_peer(direction) if axis == "z" else x_peer(direction)
        copy = remote(piece(kind, src[0], src[1], half), piece(kind, dst[0], dst[1], half), device)
        copy.start()
        flows[kind, dst, half, axis, direction] = copy

    def along_z(kind, jx, k, direction):
        slots = SLOT_UP if direction > 0 else SLOT_DOWN
        if k < 4:
            half = None if k < 3 else (0 if direction > 0 else 1)
            send(kind, "z", direction, (jx, slots[k]), (jx, slots[k + 1]), half)

    def along_x(kind, jx, slot):
        if jx == 0:
            send(kind, "x", 1, (0, slot), (1, slot), None)
            send(kind, "x", -1, (0, slot), (2, slot), None)
        elif jx == 1:
            send(kind, "x", 1, (1, slot), (3, slot), 0)
        elif jx == 2:
            send(kind, "x", -1, (2, slot), (3, slot), 1)

    def got(kind, dst, half, axis, direction):
        flows[kind, dst, half, axis, direction].wait_recv()

    def arrive(kind, jx, dz):
        k = abs(dz)
        up = dz < 0
        slot = (SLOT_UP if up else SLOT_DOWN)[k]
        z_last = kind == "d" and k > 0 or kind == "u" and jx == 0
        if z_last:
            if k == 4:
                got(kind, (jx, 7), 0, "z", 1)
                got(kind, (jx, 7), 1, "z", -1)
            else:
                got(kind, (jx, slot), None, "z", 1 if up else -1)
                along_z(kind, jx, k, 1 if up else -1)
            if kind == "u":
                along_x(kind, 0, slot)
        else:
            if jx == 3:
                got(kind, (3, slot), 0, "x", 1)
                got(kind, (3, slot), 1, "x", -1)
            else:
                got(kind, (jx, slot), None, "x", 1 if jx == 1 else -1)
                along_x(kind, jx, slot)
            if kind == "d":
                along_z(kind, jx, 0, 1)
                along_z(kind, jx, 0, -1)

    along_z("u", 0, 0, 1)
    along_z("u", 0, 0, -1)
    along_x("d", 0, 0)
    along_x("u", 0, 0)
    along_z("d", 0, 0, 1)
    along_z("d", 0, 0, -1)

    x_mate = remote(x_buf.at[0], x_buf.at[1], mate)
    x_mate.start()
    x_partner = []
    for j in range(4):
        rows = pl.ds(128 * j, 128)
        copy = remote(x_buf.at[0, rows], x_buf.at[2, rows], partner)
        copy.start()
        x_partner.append(copy)
    x_pass = []

    bias_z = []
    for k in range(1, NZ):
        slot = SLOT_UP[k] if k <= 4 else SLOT_DOWN[NZ - k]
        copy = remote(bb.at[0, 0], bb.at[0, slot], z_peer(k))
        copy.start()
        bias_z.append(copy)
    bias_x = []

    def tally(first, last):
        def body(i, carry):
            delta = codes[...] - i * 256
            total = jnp.zeros((256, 256), F32)
            for part in range(4):
                row = lax.broadcasted_iota(jnp.int32, (256, 512), 0)
                hot = jnp.where(row == delta[:, 512 * part : 512 * (part + 1)], 1.0, 0.0).astype(BF)
                total = total + jnp.dot(hot, sv[512 * part : 512 * (part + 1), :], preferred_element_type=F32)
            for j in range(2):
                here = total[128 * j : 128 * (j + 1)]
                diagonal = lax.broadcasted_iota(jnp.int32, (128, 128), 0) == lax.broadcasted_iota(
                    jnp.int32, (128, 128), 1
                )
                count = jnp.sum(jnp.where(diagonal, here[:, 128:], 0.0), axis=0, keepdims=True)
                tt[2 * i + j, 0:128, :] = here[:, :128].astype(BF)
                tt[2 * i + j, 128:144, :] = count_rows(count[None], 1)[0].astype(BF)
            return carry

        lax.fori_loop(first, last, body, 0)

    def x_blocks(k):
        return pl.multiple_of(((x + k + NX) % NX) * NZ, NZ)

    rs = {}

    def add_into(base, count, others):
        def body(i, carry):
            total = tt[pl.ds(base + i, 1)].astype(F32)
            for ref in others:
                total = total + ref[pl.ds(i, 1)].astype(F32)
            tt[pl.ds(base + i, 1)] = tidy_block(total)
            return carry

        lax.fori_loop(0, count, body, 0)

    def reduce_1():
        far = x_blocks(2)
        rs["a+"] = remote(tt.at[pl.ds(far, 4)], ra.at[0], x_peer(1))
        rs["a-"] = remote(tt.at[pl.ds(far + 4, 4)], ra.at[1], x_peer(-1))
        rs["a+"].start()
        rs["a-"].start()

    def reduce_2():
        rs["a+"].wait_recv()
        rs["a-"].wait_recv()
        add_into(x_blocks(1), 4, [ra.at[0]])
        rs["b+"] = remote(tt.at[pl.ds(x_blocks(1), 8)], rb.at[0], x_peer(1))
        rs["b+"].start()
        add_into(x_blocks(-1) + 4, 4, [ra.at[1]])
        rs["b-"] = remote(tt.at[pl.ds(x_blocks(-1), 8)], rb.at[1], x_peer(-1))
        rs["b-"].start()

    def reduce_3():
        rs["b+"].wait_recv()
        rs["b-"].wait_recv()
        add_into(x_blocks(0), 8, [rb.at[0], rb.at[1]])
        for k in (4, 3, 5, 2, 6, 1, 7):
            rs["c", k] = remote(tt.at[x_blocks(0) + (z + k) % NZ], rc.at[k - 1], z_peer(k))
            rs["c", k].start()

    def reduce_4():
        for k in range(1, NZ):
            rs["c", k].wait_recv()
        total = tt[pl.ds(x_blocks(0) + z, 1)].astype(F32)
        for k in range(1, NZ):
            total = total + rc[k - 1 : k].astype(F32)
        ff[pl.ds(x_blocks(0) + z, 1)] = tidy_block(total)
        for k in (4, 3, 5, 2, 6, 1, 7):
            mine = ff.at[x_blocks(0) + z]
            rs["f", k] = remote(mine, mine, z_peer(k))
            rs["f", k].start()

    def gather_1():
        for k in range(1, NZ):
            rs["f", k].wait_recv()
        mine = ff.at[pl.ds(x_blocks(0), 8)]
        for k in (1, -1):
            rs["g", k] = remote(mine, mine, x_peer(k))
            rs["g", k].start()

    def gather_2():
        for k, half in ((1, 0), (-1, 1)):
            rs["g", k].wait_recv()
            part = ff.at[pl.ds(x_blocks(-k) + 4 * half, 4)]
            rs["h", k] = remote(part, part, x_peer(k))
            rs["h", k].start()

    def gather_3():
        rs["h", 1].wait_recv()
        rs["h", -1].wait_recv()

    def bias_of(h, first):
        lanes = lax.broadcasted_iota(jnp.int32, (1, 128), 1) // 32
        parts = []
        for jx in (first, first + 1):
            part = jnp.zeros((1, 128), F32)
            for i in range(4):
                part = jnp.where(lanes == i, bb[jx, 4 * h + i, 0:1, :], part)
            parts.append(part)
        return jnp.concatenate(parts, axis=1)

    def forward(g, b, finish=None):
        h, first = g // 2, 2 * (g % 2)
        bias = bias_of(h, first)
        up = gu[h, first : first + 2].reshape(256, 1024)
        down = gd[h, first : first + 2].reshape(256, 1024)

        def body(i, carry):
            rows = pl.ds(pl.multiple_of(256 * i, 256), 256)
            pre = lax.dot_general(
                x_buf[b, rows, :], up, (((1,), (1,)), ((), ())), preferred_element_type=F32
            )
            hidden = gelu(pre + bias).astype(BF)
            out = jnp.dot(hidden, down, preferred_element_type=F32)
            if g > 0:
                out = out + acc[b, rows, :]
            if finish is None:
                acc[b, rows, :] = out
            else:
                ps[finish, rows, :] = out.astype(BF)
            return carry

        lax.fori_loop(0, 2, body, 0)

    rounds = {}
    for dz in (0, -1, 1, -2, 2, -3, 3, 4):
        for jx in range(4):
            reach = abs(dz) + (0, 1, 1, 2)[jx]
            if reach:
                rounds.setdefault(reach, []).append((jx, dz))

    def do_round(r):
        for kind in ("u", "d"):
            for jx, dz in rounds[r]:
                arrive(kind, jx, dz)

    def bias_spread():
        for copy in bias_z:
            copy.wait_recv()
        for k, slot in ((1, 1), (-1, 2), (2, 3)):
            copy = remote(bb.at[0], bb.at[slot], x_peer(k))
            copy.start()
            bias_x.append(copy)

    def pass_rows(first, last):
        for j in range(first, last):
            x_partner[j].wait_recv()
            rows = pl.ds(128 * j, 128)
            copy = remote(x_buf.at[2, rows], x_buf.at[3, rows], mate)
            copy.start()
            x_pass.append(copy)

    load_s.wait()
    tally(0, 5)
    do_round(1)
    bias_spread()
    tally(5, 12)
    do_round(2)
    tally(12, 16)
    reduce_1()
    pass_rows(0, 2)
    do_round(3)
    pass_rows(2, 3)
    x_mate.wait_recv()
    for copy in bias_x:
        copy.wait_recv()
    forward(0, 0)
    reduce_2()
    forward(0, 1)
    do_round(4)
    pass_rows(3, 4)
    forward(1, 0)
    forward(1, 1)
    reduce_3()
    for copy in x_pass:
        copy.wait_recv()
    forward(0, 2)
    forward(0, 3)
    do_round(5)
    forward(1, 2)
    forward(1, 3)
    forward(2, 3)
    forward(2, 2)
    reduce_4()
    forward(2, 1)
    forward(2, 0)
    do_round(6)

    forward(3, 3, 0)
    to_mate_3 = remote(ps.at[0], pr.at[0], mate)
    to_mate_3.start()
    forward(3, 2)
    to_mate_3.wait_recv()
    to_partner = []
    for j in range(4):
        rows = pl.ds(128 * j, 128)
        ps[1, rows, :] = (acc[2, rows, :] + pr[0, rows, :].astype(F32)).astype(BF)
        copy = remote(ps.at[1, rows], pr.at[2, rows], partner)
        copy.start()
        to_partner.append(copy)
    forward(3, 1, 2)
    to_mate_1 = remote(ps.at[2], pr.at[1], mate)
    to_mate_1.start()
    forward(3, 0)
    gather_1()
    to_mate_1.wait_recv()

    ends = [lengths[0, 0, 0]]
    for p in range(1, 4):
        ends.append(ends[-1] + lengths[0, 0, p])
    row8 = lax.broadcasted_iota(jnp.int32, (8, 1), 0)
    opening = jnp.full((8, 1), 0, jnp.int32)
    ending = jnp.full((8, 1), 0, jnp.int32)
    size = jnp.full((8, 1), 1, jnp.int32)
    for p in range(4):
        opening = jnp.where(row8 == p, ends[p] - lengths[0, 0, p], opening)
        ending = jnp.where(row8 == p, ends[p], ending)
        size = jnp.where(row8 == p, lengths[0, 0, p], size)

    pooled[...] = jnp.zeros((8, 1024), F32)
    for j in range(4):
        to_partner[j].wait_recv()
        rows = pl.ds(128 * j, 128)
        resid = (
            x_buf[0, rows, :].astype(F32)
            + (acc[0, rows, :] + pr[1, rows, :].astype(F32) + pr[2, rows, :].astype(F32))
            + down_bias[...]
        )
        center = resid - jnp.mean(resid, axis=-1, keepdims=True)
        spread = jnp.mean(center * center, axis=-1, keepdims=True)
        layer_out = (center * lax.rsqrt(spread + 1e-12) * ln_gain[...] + ln_bias[...]).astype(BF)
        place = lax.broadcasted_iota(jnp.int32, (8, 128), 1) + 128 * j
        member = jnp.where((place >= opening) & (place < ending), 1.0, 0.0).astype(BF)
        pooled[...] += jnp.dot(member, layer_out, preferred_element_type=F32)
        if j == 1:
            gather_2()
    mean = pooled[...] / size.astype(F32)
    scaling = lax.rsqrt(jnp.mean(mean * mean, axis=-1, keepdims=True) + 1e-06)
    embedded = (mean * scaling).astype(BF).astype(F32)
    for i in range(NS):
        em[i] = embedded[:, 128 * i : 128 * (i + 1)]

    to_owner = []
    for k in range(1, NS):
        copy = remote(em.at[(s + k) % NS], er.at[s], s_peer(k))
        copy.start()
        to_owner.append(copy)
    er[pl.ds(s, 1)] = em[pl.ds(s, 1)]
    gather_3()
    save_f = local(ff, f_out)
    for copy in to_owner:
        copy.wait_recv()
    low = lax.broadcasted_iota(jnp.int32, (8, 128), 0) < 4
    tiles = [jnp.where(low, er[2 * i], pltpu.roll(er[2 * i + 1], 4, 0)) for i in range(4)]
    ee[x, z] = jnp.concatenate(tiles, axis=0).astype(BF)

    e_copies = []
    for k in (4, 3, 5, 2, 6, 1, 7):
        copy = remote(ee.at[x, z], ee.at[x, z], z_peer(k))
        copy.start()
        e_copies.append(copy)
    for copy in e_copies:
        copy.wait_recv()
    e_copies = []
    for k in (2, 1, 3):
        copy = remote(ee.at[x], ee.at[x], x_peer(k))
        copy.start()
        e_copies.append(copy)
    for copy in e_copies:
        copy.wait_recv()
    saves = [local(ee.at[i], e_out.at[:, i]) for i in range(NX)]
    for copy in started:
        copy.wait_send()
    save_f.wait()
    for copy in saves:
        copy.wait()


def update_kernel(e_all, new_codes, table, centroids, embeds, updated, right):
    i = pl.program_id(0)

    @pl.when(i == 0)
    def _():
        right[0:1024, 0:128] = e_all[...]
        right[0:1024, 128:256] = jnp.ones((1024, 128), BF)
        lanes = lax.broadcasted_iota(jnp.int32, (128, 256), 1)
        right[1024:1152, :] = jnp.where(lanes >= 128, 256.0, 0.0).astype(BF)
        right[1152:1280, :] = jnp.where(lanes >= 128, 1.0, 0.0).astype(BF)
        mine = pl.multiple_of(lax.axis_index("dp") * 32, 32)
        embeds[...] = e_all[pl.ds(mine, 32), :]

    diagonal = lax.broadcasted_iota(jnp.int32, (128, 128), 0) == lax.broadcasted_iota(
        jnp.int32, (128, 128), 1
    )
    row = lax.broadcasted_iota(jnp.int32, (128, 1024), 0)
    for j in range(4):
        rows = pl.ds(128 * j, 128)
        delta = new_codes[...] - (i * 512 + 128 * j)
        hot = jnp.where(row == delta, 1.0, 0.0).astype(BF)
        high = jnp.where(diagonal, table[j, 128:129, :].astype(F32), 0.0).astype(BF)
        low = jnp.where(diagonal, table[j, 129:130, :].astype(F32), 0.0).astype(BF)
        left = jnp.concatenate([hot, high, low], axis=1)
        new = jnp.dot(left, right[...], preferred_element_type=F32)
        total = table[j, 0:128, :].astype(F32) + new[:, :128] + centroids[0, rows, :]
        updated[0, rows, :] = total / (new[:, 128:] + 1.0)


def on_device(
    tokens, lengths, w_up, up_bias, w_down, down_bias, ln_gain, ln_bias, stored, stored_codes, new_codes, centroids
):
    vmem = pl.BlockSpec(memory_space=pltpu.VMEM)
    smem = pl.BlockSpec(memory_space=pltpu.SMEM)
    hbm = pl.BlockSpec(memory_space=pl.ANY)
    e_all, table = pl.pallas_call(
        layer_kernel,
        out_shape=(
            jax.ShapeDtypeStruct((NZ, NX, 32, 128), BF),
            jax.ShapeDtypeStruct((32, 144, 128), BF),
        ),
        in_specs=[hbm, hbm, hbm, hbm, smem, vmem, vmem, vmem, vmem, vmem],
        out_specs=(hbm, hbm),
        scratch_shapes=[
            pltpu.VMEM((4, 512, 1024), BF),
            pltpu.VMEM((2, 4, 4, 32, 1024), BF),
            pltpu.VMEM((2, 4, 4, 32, 1024), BF),
            pltpu.VMEM((4, 512, 1024), F32),
            pltpu.VMEM((3, 512, 1024), BF),
            pltpu.VMEM((3, 512, 1024), BF),
            pltpu.VMEM((2048, 256), BF),
            pltpu.VMEM((32, 144, 128), BF),
            pltpu.VMEM((2, 4, 144, 128), BF),
            pltpu.VMEM((2, 8, 144, 128), BF),
            pltpu.VMEM((7, 144, 128), BF),
            pltpu.VMEM((32, 144, 128), BF),
            pltpu.VMEM((4, 8, 8, 128), F32),
            pltpu.VMEM((8, 8, 128), F32),
            pltpu.VMEM((8, 8, 128), F32),
            pltpu.VMEM((NX, NZ, 32, 128), BF),
            pltpu.VMEM((8, 1024), F32),
            pltpu.SemaphoreType.DMA((256,)),
            pltpu.SemaphoreType.DMA((256,)),
            pltpu.SemaphoreType.DMA((16,)),
        ],
        compiler_params=pltpu.CompilerParams(
            collective_id=0, has_side_effects=True, vmem_limit_bytes=52 * 1024 * 1024
        ),
    )(
        tokens, w_up, w_down, stored, lengths, up_bias.reshape(1, 128), down_bias.reshape(1, 1024),
        ln_gain.reshape(1, 1024), ln_bias.reshape(1, 1024), stored_codes,
    )
    embeds, updated = pl.pallas_call(
        update_kernel,
        grid=(8,),
        out_shape=(
            jax.ShapeDtypeStruct((32, 128), BF),
            jax.ShapeDtypeStruct((1, 4096, 128), F32),
        ),
        in_specs=[
            pl.BlockSpec((1024, 128), lambda i: (0, 0)),
            pl.BlockSpec((1, 1024), lambda i: (0, 0)),
            pl.BlockSpec((4, 144, 128), lambda i: (i, 0, 0)),
            pl.BlockSpec((1, 512, 128), lambda i: (0, i, 0)),
        ],
        out_specs=(
            pl.BlockSpec((32, 128), lambda i: (0, 0)),
            pl.BlockSpec((1, 512, 128), lambda i: (0, i, 0)),
        ),
        scratch_shapes=[pltpu.VMEM((1280, 256), BF)],
        compiler_params=pltpu.CompilerParams(vmem_limit_bytes=32 * 1024 * 1024),
    )(e_all.reshape(1024, 128), new_codes, table, centroids)
    return embeds, updated


def solution(mesh):
    return jax.shard_map(
        on_device,
        mesh=mesh,
        in_specs=(
            P(("dp", "sub"), None),
            P("dp", "sub", None),
            P("dp", None),
            P("dp"),
            P("dp", None),
            P(),
            P(),
            P(),
            P("dp", "sub"),
            P("sub", "dp"),
            P("sub", None),
            P("sub", None, None),
        ),
        out_specs=(P("dp", "sub"), P("sub", None, None)),
        check_vma=False,
    )
```

time: 441 us -> 108 us (0.24)
  waiting for transfers between devices: 199 us -> 0 us
  blocking collectives: 147 us -> 0 us
  Pallas kernels: 0 us -> 98.1 us
  matrix products: 45.1 us -> 0 us
  other arithmetic: 14 us -> 0 us
  between operations: 13.8 us -> 0.69 us
  loops' own time: 5.45 us -> 0 us
  starting transfers between devices: 5.43 us -> 0 us
    all_gather x2 -> x0, waiting for transfers between devices: 164 us -> none  [the longest x1 98 us: on_device(): down_rows = lax.all_gather(w_down, 'dp', axis=0, tiled=True)]
    psum x1 -> x0, blocking collectives: 112 us -> none  [on_device(): lax.psum(counts.astype(jnp.bfloat16), 'dp').astype(jnp.float32)]
    pallas_call x0 -> x2, Pallas kernels: none -> 98.1 us  [the longest x1 92.5 us: on_device(): pl.pallas_call(layer_kernel, out_shape=(jax.ShapeDtypeStruct((NZ, NX, 32,...]
    dot_general x10 -> x0, matrix products: 45.1 us -> none  [the longest x1 30.8 us: on_device(): ffn_total = jnp.dot(hidden, down_rows, preferred_element_type=jnp.float32)]
    all_gather x1 -> x0, blocking collectives: 35.5 us -> none  [on_device(): bias_matrix_rows = lax.all_gather(up_bias, 'dp', axis=0, tiled=True)]
    psum x1 -> x0, waiting for transfers between devices: 29.1 us -> none  [on_device(): lax.psum(centroid_totals.astype(jnp.bfloat16), 'dp').astype(jnp.float32)]
    reduce_sum x9 -> x0, other arithmetic: 8.12 us -> none  [the longest x8 7.77 us: one_group(): counts = jnp.sum(assignment_matrix, axis=2, dtype=jnp.float32)]
    unnamed x15 -> x24, local copies, waits for them, and re-layouts: 1.58 us -> 8.42 us
  transfers between devices with their start and end apart: 4 -> 0, of which waited for: 4 -> 0; matrix products, arithmetic and copies ran while one was open for 1% -> 0% of each run, Pallas kernels for 0% -> 0%
where the time goes in v1:
time: 108 us; the launch traced here: 107 us
  Pallas kernels  98.1 us (91%)
  local copies, waits for them, and re-layouts  8.42 us (8%)
    pallas_call x1, Pallas kernels, on_device(): pl.pallas_call(layer_kernel, out_shape=(jax.ShapeDtypeStruct((NZ, NX, 32,...  92.5 us
    unnamed x24, local copies, waits for them, and re-layouts  8.42 us
    pallas_call x1, Pallas kernels, on_device(): pl.pallas_call(update_kernel, grid=(8,), out_shape=(jax.ShapeDtypeStruct(...  5.58 us

profile of v1, /device:TPU:1, one launch (start us, length us, event | category | flops | bytes accessed | tf_op | source)
XLA Modules:
  0.0 107.2 jit_solution(16130998638269052826)
XLA Ops:
  0.6 0.0 copy-start
  0.6 0.0 copy-start.2
  0.7 1.2 %copy-done.2 = bf16[2048,128]{1,0:T(8,128)(2,1)S(1)} copy-done((bf16[2048,128]{1,0:T(8,128)(2,1)S(1)}, bf16[2048,128]{1,0:T(8,128)(2,1)}, u32[]{:S(2)}) %copy-start.2) | copy-done | bytes 524312
  1.8 0.0 copy-start.3
  1.8 0.9 copy-done.3
  2.8 0.0 copy-start.4
  2.8 0.9 copy-done.4
  3.7 0.0 copy-start.5
  3.7 0.7 copy-done.5
  4.4 0.0 copy-start.6
  4.4 0.7 copy-done.6
  5.1 0.0 copy-start.7
  5.1 0.7 copy-done.7
  5.8 0.0 copy-start.8
  5.8 0.7 copy-done.8
  6.5 0.0 copy-start.10
  6.5 0.7 copy-done.10
  7.2 0.0 copy-start.11
  7.2 0.7 copy-done.11
  7.8 0.0 copy-start.9
  7.8 92.5 %shard_map.131 = (bf16[8,4,32,128]{3,2,1,0:T(8,128)(2,1)S(1)}, bf16[32,144,128]{2,1,0:T(8,128)(2,1)}) custom-call(bf16[512,1024]{1,0:T(8,128)(2,1)} %tokens.1, bf16[128,1024]{1,0:T(8,128)(2,1)S(1)} %copy-done.3, bf16[128,1024]{1,0:T(8,128)(2,1)S(1)} %copy-done.4, bf16[2048,128]{1,0:T(8,128)(2,1)S(1)} %copy-done.2, s32[1,1,4]{2,1,0:T(1,128)S(1)} %copy-done.10, ...), custom_call_target="tpu_custom_call" | custom-call | tf_op jit(solution)/shard_map/pallas_call | solution.py:509
  100.4 0.0 copy-done
  100.4 0.0 copy-done.9
  100.4 0.0 copy-start.1
  100.4 1.3 %copy-done.1 = bf16[32,144,128]{2,1,0:T(8,128)(2,1)S(1)} copy-done((bf16[32,144,128]{2,1,0:T(8,128)(2,1)S(1)}, bf16[32,144,128]{2,1,0:T(8,128)(2,1)}, u32[]{:S(2)}) %copy-start.1) | copy-done | bytes 1179672
  101.6 5.6 %shard_map.132 = (bf16[32,128]{1,0:T(8,128)(2,1)}, f32[1,4096,128]{2,1,0:T(8,128)}) custom-call(bf16[1024,128]{1,0:T(8,128)(2,1)S(1)} %bitcast.5, s32[1,1024]{1,0:T(1,128)S(1)} %copy-done.9, bf16[32,144,128]{2,1,0:T(8,128)(2,1)S(1)} %copy-done.1, f32[1,4096,128]{2,1,0:T(8,128)S(1)} %copy-done), custom_call_target="tpu_custom_call" | custom-call | tf_op jit(solution)/shard_map/pallas_call | solution.py:546
Async XLA Ops:
  0.6 99.7 %copy-start = (f32[1,4096,128]{2,1,0:T(8,128)S(1)}, f32[1,4096,128]{2,1,0:T(8,128)}, u32[]{:S(2)}) copy-start(f32[1,4096,128]{2,1,0:T(8,128)} %centroids.1) | copy-start | bytes 6291460
  0.6 1.2 %copy-start.2 = (bf16[2048,128]{1,0:T(8,128)(2,1)S(1)}, bf16[2048,128]{1,0:T(8,128)(2,1)}, u32[]{:S(2)}) copy-start(bf16[2048,128]{1,0:T(8,128)(2,1)} %stored.1) | copy-start | bytes 1572868
  1.8 0.9 copy-start.3
  2.8 0.9 copy-start.4
  3.7 0.7 copy-start.5
  4.4 0.7 copy-start.6
  5.1 0.7 copy-start.7
  5.8 0.7 copy-start.8
  6.5 0.7 copy-start.10
  7.2 0.7 copy-start.11
  7.8 92.6 %copy-start.9 = (s32[1,1024]{1,0:T(1,128)S(1)}, s32[1,1024]{1,0:T(1,128)}, u32[]{:S(2)}) copy-start(s32[1,1024]{1,0:T(1,128)} %new_codes.1) | copy-start | bytes 12292
  100.4 1.3 %copy-start.1 = (bf16[32,144,128]{2,1,0:T(8,128)(2,1)S(1)}, bf16[32,144,128]{2,1,0:T(8,128)(2,1)}, u32[]{:S(2)}) copy-start(bf16[32,144,128]{2,1,0:T(8,128)(2,1)} %get-tuple-element.5.table) | copy-start | bytes 3538948

commit v2 on v0

v2 whole, which is shorter than its diff:
```python
import functools

import jax
import jax.numpy as jnp
from jax import lax
from jax.experimental import pallas as pl
from jax.experimental.pallas import tpu as pltpu
from jax.sharding import PartitionSpec as P

MESH = pl.DeviceIdType.MESH
NX, NZ, NS = 4, 8, 8
BF, F32 = jnp.bfloat16, jnp.float32

GELU_P = (
    0.7978849411010742,
    0.03633308410644531,
    -3.259497316321358e-05,
    -5.530619455385022e-05,
    3.964744792028796e-06,
    -1.322633664813111e-07,
    1.7561715415226331e-09,
)
GELU_CAP = 30.0

SLOT_UP = (0, 1, 3, 5, 7)
SLOT_DOWN = (0, 2, 4, 6, 7)


ORDER = (
    101, 111, 340, 341, 354, 370, 201, 211, 352, 353, 355, 350, 313, 303, 0, 1, 2, 3, 4, 340, 342, 221, 231, 341,
    343, 241, 251, 370, 371, 350, 5, 101, 102, 302, 312, 111, 112, 304, 314, 201, 202, 211, 212, 313, 333, 303, 323,
    6, 7, 373, 372, 342, 343, 261, 271, 231, 232, 221, 222, 251, 252, 241, 242, 333, 323, 371, 354, 358, 302, 322,
    102, 103, 301, 311, 112, 113, 305, 315, 202, 203, 212, 213, 352, 356, 353, 357, 355, 359, 312, 332, 304, 324,
    314, 334, 358, 261, 262, 271, 272, 372, 373, 9, 375, 8, 374, 356, 357, 359, 222, 223, 232, 233, 322, 252, 253,
    242, 243, 324, 332, 334, 301, 321, 23, 213, 214, 103, 104, 300, 310, 113, 114, 316, 306, 203, 204, 311, 331,
    305, 325, 315, 335, 22, 272, 273, 262, 263, 21, 223, 224, 233, 234, 20, 321, 243, 244, 253, 254, 104, 214, 204,
    114, 307, 317, 325, 273, 274, 263, 264, 331, 27, 335, 224, 234, 244, 254, 26, 300, 320, 306, 326, 25, 274, 316,
    336, 264, 310, 330, 24, 307, 327, 317, 337, 31, 375, 374, 10, 380, 29, 320, 326, 30, 336, 330, 327, 337, 28, 46,
    364, 47, 365, 44, 45, 42, 366, 43, 367, 40, 41, 364, 51, 361, 50, 360, 380, 11, 381, 365, 52, 362, 53, 363, 366,
    367, 381, 376, 377, 361, 360, 54, 55, 362, 363, 56, 57, 58, 382, 382, 59, 400, 393, 395, 392, 396, 394, 391,
    397, 376, 378, 377, 379, 400, 391, 401, 397, 407, 392, 402, 396, 406, 393, 403, 395, 405, 394, 404, 401, 407,
    402, 406, 403, 405, 404, 378, 379,
)


def gelu(p):
    t = jnp.minimum(p * p, GELU_CAP)
    q = jnp.full_like(t, GELU_P[-1])
    for coefficient in GELU_P[-2::-1]:
        q = q * t + coefficient
    half = 0.5 * p
    return half + half * jnp.tanh(p * q)


def tidy_block(total):
    n = total.shape[0]
    count = 256.0 * total[:, 128:129, :] + total[:, 129:130, :]
    return jnp.concatenate([total[:, :128, :], count_rows(count, n)], axis=1).astype(BF)


def count_rows(count, n):
    high = jnp.floor(count * (1.0 / 256.0))
    low = count - 256.0 * high
    row = lax.broadcasted_iota(jnp.int32, (n, 16, 128), 1)
    return jnp.where(row == 0, high, jnp.where(row == 1, low, 0.0))


def layer_kernel(
    tokens, w_up, w_down, stored, lengths_in, up_bias_in, down_bias_in, ln_gain_in, ln_bias_in, codes_in,
    e_out, f_out, lengths, up_bias, down_bias, ln_gain, ln_bias, codes,
    x_buf, gu, gd, acc, ps, pr, sv, tt, ra, rb, rc, ff, bb, em, er, ee, pooled,
    send_sem, recv_sem, local_sem,
):
    dp, s = lax.axis_index("dp"), lax.axis_index("sub")
    z, x, core = dp // NX, dp % NX, s % 2
    quarter = ((s // 2) % 2) * 2 + core

    def z_peer(k):
        return (((z + k + NZ) % NZ) * NX + x, s)

    def x_peer(k):
        return (z * NX + (x + k + NX) % NX, s)

    def s_peer(k):
        return (dp, (s + k) % NS)

    mate = (dp, s + 1 - 2 * core)
    partner = (dp, (s + 2 * core - 1 + NS) % NS)

    used = [0]
    sent = {}

    def remote(src, dst, device, arrival):
        return pltpu.make_async_remote_copy(
            src_ref=src, dst_ref=dst, send_sem=send_sem, recv_sem=arrival,
            device_id=device, device_id_type=MESH,
        )

    def local(src, dst):
        i = used[0]
        used[0] += 1
        copy = pltpu.make_async_copy(src, dst, local_sem.at[i])
        copy.start()
        return copy

    barrier = pltpu.get_barrier_semaphore()
    peers = [z_peer(k) for k in range(1, NZ)] + [x_peer(k) for k in range(1, NX)] + [s_peer(k) for k in range(1, NS)]
    for device in peers:
        pl.semaphore_signal(barrier, inc=1, device_id=device, device_id_type=MESH)

    row0 = pl.multiple_of(quarter * 32, 32)
    load_up = local(w_up.at[pl.ds(row0, 32)], gu.at[0, 0, 0])
    load_down = local(w_down.at[pl.ds(row0, 32)], gd.at[0, 0, 0])
    load_x = local(tokens, x_buf.at[0])
    load_bias = local(up_bias_in, up_bias)
    load_codes = local(codes_in, codes)
    load_s = local(stored, sv.at[:, pl.ds(0, 128)])
    load_rest = [local(lengths_in, lengths), local(down_bias_in, down_bias), local(ln_gain_in, ln_gain), local(ln_bias_in, ln_bias)]
    load_bias.wait()
    lane = lax.broadcasted_iota(jnp.int32, (8, 128), 1)
    own_bias = jnp.where(lane // 32 == quarter, jnp.broadcast_to(up_bias[...].astype(F32), (8, 128)), 0.0)
    own_bias = own_bias + pltpu.roll(own_bias, 64, 1)
    bb[0, 0] = own_bias + pltpu.roll(own_bias, 32, 1)
    sv[:, 128:256] = jnp.ones((2048, 128), BF)

    load_up.wait()
    load_down.wait()
    load_x.wait()
    pl.semaphore_wait(barrier, len(peers))

    copies = {}

    def piece(buffer, jx, slot, half=None):
        ref = buffer.at[slot // 4, jx, slot % 4]
        return ref if half is None else ref.at[pl.ds(16 * half, 16)]

    ways = ((1, SLOT_UP, 0), (-1, SLOT_DOWN, 1))
    for way, slots, half in ways:
        for k in range(1, 5):
            part = half if k == 4 else None
            copies[100 + 10 * half + k] = [
                (piece(gu, 0, slots[k - 1], part), piece(gu, 0, slots[k], part), z_peer(way))
            ]
            for jx in range(4):
                copies[200 + 20 * jx + 10 * half + k] = [
                    (piece(gd, jx, slots[k - 1], part), piece(gd, jx, slots[k], part), z_peer(way))
                ]
        near = 1 if way > 0 else 2
        for dz in range(-3, 5):
            slot = SLOT_UP[-dz] if dz < 0 else SLOT_DOWN[dz]
            copies[303 + 10 * half + dz] = [(piece(gu, 0, slot), piece(gu, near, slot), x_peer(way))]
            copies[323 + 10 * half + dz] = [(piece(gu, near, slot, half), piece(gu, 3, slot, half), x_peer(way))]
        copies[340 + half] = [(piece(gd, 0, 0), piece(gd, near, 0), x_peer(way))]
        copies[342 + half] = [(piece(gd, near, 0, half), piece(gd, 3, 0, half), x_peer(way))]

    def part_of(ref, j, size):
        return ref.at[pl.ds(size * j, size)]

    copies[350] = [(x_buf.at[0], x_buf.at[1], mate)]
    for j in range(4):
        copies[352 + j] = [(part_of(x_buf.at[0], j, 128), part_of(x_buf.at[2], j, 128), partner)]
        copies[356 + j] = [(part_of(x_buf.at[2], j, 128), part_of(x_buf.at[3], j, 128), mate)]
        copies[360 + j] = [(part_of(ps.at[1], j, 128), part_of(pr.at[2], j, 128), partner)]
    for i in range(2):
        copies[364 + i] = [(part_of(ps.at[0], i, 256), part_of(pr.at[0], i, 256), mate)]
        copies[366 + i] = [(part_of(ps.at[2], i, 256), part_of(pr.at[1], i, 256), mate)]
    copies[370] = [
        (bb.at[0, 0], bb.at[0, SLOT_UP[k] if k <= 4 else SLOT_DOWN[NZ - k]], z_peer(k)) for k in range(1, NZ)
    ]
    copies[371] = [(bb.at[0], bb.at[slot], x_peer(k)) for k, slot in ((1, 1), (-1, 2), (2, 3))]

    def x_blocks(k):
        return pl.multiple_of(((x + k + NX) % NX) * NZ, NZ)

    far, own = x_blocks(2), x_blocks(0)
    for way, slots, half in ways:
        copies[372 + half] = [(tt.at[pl.ds(far + 4 * half, 4)], ra.at[half], x_peer(way))]
        copies[374 + half] = [(tt.at[pl.ds(x_blocks(way), 8)], rb.at[half], x_peer(way))]
        copies[376 + half] = [(ff.at[pl.ds(own, 8)], ff.at[pl.ds(own, 8)], x_peer(way))]
        passed = ff.at[pl.ds(x_blocks(-way) + 4 * half, 4)]
        copies[378 + half] = [(passed, passed, x_peer(way))]
    copies[380] = [(tt.at[own + (z + k) % NZ], rc.at[k - 1], z_peer(k)) for k in range(1, NZ)]
    copies[381] = [(ff.at[own + z], ff.at[own + z], z_peer(k)) for k in range(1, NZ)]
    copies[382] = [(em.at[(s + k) % NS], er.at[s], s_peer(k)) for k in range(1, NS)]
    for k in range(NZ):
        row = (z - k + NZ) % NZ
        if k:
            copies[390 + k] = [(ee.at[x, z], ee.at[x, z], z_peer(k))]
        copies[400 + k] = [(ee.at[x, row], ee.at[x, row], x_peer(j)) for j in (2, 1, 3)]

    compute = {}

    def tally(first, last):
        def body(i, carry):
            delta = codes[...] - i * 256
            total = jnp.zeros((256, 256), F32)
            for part in range(4):
                row = lax.broadcasted_iota(jnp.int32, (256, 512), 0)
                hot = jnp.where(row == delta[:, 512 * part : 512 * (part + 1)], 1.0, 0.0).astype(BF)
                total = total + jnp.dot(hot, sv[512 * part : 512 * (part + 1), :], preferred_element_type=F32)
            for j in range(2):
                here = total[128 * j : 128 * (j + 1)]
                diagonal = lax.broadcasted_iota(jnp.int32, (128, 128), 0) == lax.broadcasted_iota(
                    jnp.int32, (128, 128), 1
                )
                count = jnp.sum(jnp.where(diagonal, here[:, 128:], 0.0), axis=0, keepdims=True)
                tt[2 * i + j, 0:128, :] = here[:, :128].astype(BF)
                tt[2 * i + j, 128:144, :] = count_rows(count[None], 1)[0].astype(BF)
            return carry

        lax.fori_loop(first, last, body, 0)

    for i in range(8):
        compute[i] = functools.partial(tally, 2 * i, 2 * i + 2)

    def add_into(base, count, others):
        def body(i, carry):
            total = tt[pl.ds(base + i, 1)].astype(F32)
            for ref in others:
                total = total + ref[pl.ds(i, 1)].astype(F32)
            tt[pl.ds(base + i, 1)] = tidy_block(total)
            return carry

        lax.fori_loop(0, count, body, 0)

    compute[8] = lambda: add_into(x_blocks(1), 4, [ra.at[0]])
    compute[9] = lambda: add_into(x_blocks(-1) + 4, 4, [ra.at[1]])
    compute[10] = lambda: add_into(own, 8, [rb.at[0], rb.at[1]])

    def add_z():
        total = tt[pl.ds(own + z, 1)].astype(F32)
        for k in range(1, NZ):
            total = total + rc[k - 1 : k].astype(F32)
        ff[pl.ds(own + z, 1)] = tidy_block(total)

    compute[11] = add_z

    def bias_of(h, first):
        lanes = lax.broadcasted_iota(jnp.int32, (1, 128), 1) // 32
        parts = []
        for jx in (first, first + 1):
            part = jnp.zeros((1, 128), F32)
            for i in range(4):
                part = jnp.where(lanes == i, bb[jx, 4 * h + i, 0:1, :], part)
            parts.append(part)
        return jnp.concatenate(parts, axis=1)

    def forward_tile(g, b, i, finish=None):
        h, first = g // 2, 2 * (g % 2)
        rows = pl.ds(256 * i, 256)
        up = gu[h, first : first + 2].reshape(256, 1024)
        down = gd[h, first : first + 2].reshape(256, 1024)
        pre = lax.dot_general(x_buf[b, rows, :], up, (((1,), (1,)), ((), ())), preferred_element_type=F32)
        hidden = gelu(pre + bias_of(h, first)).astype(BF)
        out = jnp.dot(hidden, down, preferred_element_type=F32)
        if g > 0:
            out = out + acc[b, rows, :]
        if finish is None:
            acc[b, rows, :] = out
        else:
            ps[finish, rows, :] = out.astype(BF)

    def forward(g, b):
        for i in range(2):
            forward_tile(g, b, i)

    for b in range(4):
        for g in range(3):
            compute[20 + 4 * g + b] = functools.partial(forward, g, b)
        for i in range(2):
            compute[40 + 2 * b + i] = functools.partial(forward_tile, 3, b, i, {3: 0, 1: 2}.get(b))

    def add_mate(j):
        rows = pl.ds(128 * j, 128)
        ps[1, rows, :] = (acc[2, rows, :] + pr[0, rows, :].astype(F32)).astype(BF)

    def place_of_passages():
        ends = [lengths[0, 0, 0]]
        for p in range(1, 4):
            ends.append(ends[-1] + lengths[0, 0, p])
        row8 = lax.broadcasted_iota(jnp.int32, (8, 1), 0)
        opening = jnp.full((8, 1), 0, jnp.int32)
        ending = jnp.full((8, 1), 0, jnp.int32)
        size = jnp.full((8, 1), 1, jnp.int32)
        for p in range(4):
            opening = jnp.where(row8 == p, ends[p] - lengths[0, 0, p], opening)
            ending = jnp.where(row8 == p, ends[p], ending)
            size = jnp.where(row8 == p, lengths[0, 0, p], size)
        return opening, ending, size

    def norm_rows(j):
        if j == 0:
            pooled[...] = jnp.zeros((8, 1024), F32)
        opening, ending, _ = place_of_passages()
        rows = pl.ds(128 * j, 128)
        resid = (
            x_buf[0, rows, :].astype(F32)
            + (acc[0, rows, :] + pr[1, rows, :].astype(F32) + pr[2, rows, :].astype(F32))
            + down_bias[...]
        )
        center = resid - jnp.mean(resid, axis=-1, keepdims=True)
        spread = jnp.mean(center * center, axis=-1, keepdims=True)
        layer_out = (center * lax.rsqrt(spread + 1e-12) * ln_gain[...] + ln_bias[...]).astype(BF)
        place = lax.broadcasted_iota(jnp.int32, (8, 128), 1) + 128 * j
        member = jnp.where((place >= opening) & (place < ending), 1.0, 0.0).astype(BF)
        pooled[...] += jnp.dot(member, layer_out, preferred_element_type=F32)

    for j in range(4):
        compute[50 + j] = functools.partial(add_mate, j)
        compute[54 + j] = functools.partial(norm_rows, j)

    def embed():
        _, _, size = place_of_passages()
        mean = pooled[...] / size.astype(F32)
        scaling = lax.rsqrt(jnp.mean(mean * mean, axis=-1, keepdims=True) + 1e-06)
        embedded = (mean * scaling).astype(BF).astype(F32)
        for i in range(NS):
            em[i] = embedded[:, 128 * i : 128 * (i + 1)]
        er[pl.ds(s, 1)] = em[pl.ds(s, 1)]

    def own_rows():
        low = lax.broadcasted_iota(jnp.int32, (8, 128), 0) < 4
        tiles = [jnp.where(low, er[2 * i], pltpu.roll(er[2 * i + 1], 4, 0)) for i in range(4)]
        ee[x, z] = jnp.concatenate(tiles, axis=0).astype(BF)

    compute[58] = embed
    compute[59] = own_rows

    landing = {
        370: bb.at[0, pl.ds(1, 7)], 371: bb.at[pl.ds(1, 3)], 380: rc, 381: rc, 382: er.at[pl.ds(1, 7)],
    }
    load_codes.wait()
    load_s.wait()
    for copy in load_rest:
        copy.wait()
    running = {}
    for name in ORDER:
        if name in running:
            running[name].wait_recv()
        elif name in copies:
            arrival = recv_sem.at[len(running)]
            for source, target, device in copies[name]:
                copy = remote(source, target, device, arrival)
                copy.start()
            if len(copies[name]) > 1:
                whole = landing.get(name)
                if whole is None:
                    whole = ee.at[0, pl.ds(0, 3)]
                copy = remote(whole, whole, device, arrival)
            running[name] = copy
        else:
            compute[name]()
    saves = [local(ff, f_out)] + [local(ee.at[i], e_out.at[:, i]) for i in range(NX)]
    total = 0
    for ends in copies.values():
        for source, _, _ in ends:
            total += source.size * source.dtype.itemsize
    for whole in (acc, x_buf, sv):
        size = whole.size * whole.dtype.itemsize
        for _ in range(total // size):
            pltpu.make_async_copy(whole, whole, send_sem).wait()
        total %= size
    rows = pl.ds(0, total // 32768 * 16)
    pltpu.make_async_copy(ps.at[0, rows], ps.at[0, rows], send_sem).wait()
    if total % 32768:
        tiles = pl.ds(0, total % 32768 // 4096)
        pltpu.make_async_copy(er.at[tiles], er.at[tiles], send_sem).wait()
    for copy in saves:
        copy.wait()


def update_kernel(
    e_in, codes_in, table_in, centroids_in, embeds, updated,
    e_all, new_codes, table, centroids, result, right, load_sem, save_sem,
):
    def load(i, source, target):
        copy = pltpu.make_async_copy(source, target, load_sem.at[i])
        copy.start()
        return copy

    first = [load(0, codes_in, new_codes), load(1, e_in, e_all)]
    parts = []
    for i in range(8):
        blocks, rows = pl.ds(4 * i, 4), pl.ds(512 * i, 512)
        parts.append(
            [
                load(2 + 2 * i, table_in.at[blocks], table.at[blocks]),
                load(3 + 2 * i, centroids_in.at[0, rows], centroids.at[rows]),
            ]
        )
    right[0:1024, 128:256] = jnp.ones((1024, 128), BF)
    lanes = lax.broadcasted_iota(jnp.int32, (128, 256), 1)
    right[1024:1152, :] = jnp.where(lanes >= 128, 256.0, 0.0).astype(BF)
    right[1152:1280, :] = jnp.where(lanes >= 128, 1.0, 0.0).astype(BF)
    diagonal = lax.broadcasted_iota(jnp.int32, (128, 128), 0) == lax.broadcasted_iota(
        jnp.int32, (128, 128), 1
    )
    row = lax.broadcasted_iota(jnp.int32, (128, 1024), 0)
    for copy in first:
        copy.wait()
    right[0:1024, 0:128] = e_all[...]
    mine = pl.multiple_of(lax.axis_index("dp") * 32, 32)
    save_own = pltpu.make_async_copy(e_all.at[pl.ds(mine, 32)], embeds, load_sem.at[0])
    save_own.start()
    saves = []
    for i in range(8):
        for copy in parts[i]:
            copy.wait()
        for j in range(4 * i, 4 * i + 4):
            rows = pl.ds(128 * j, 128)
            hot = jnp.where(row == new_codes[...] - 128 * j, 1.0, 0.0).astype(BF)
            high = jnp.where(diagonal, table[j, 128:129, :].astype(F32), 0.0).astype(BF)
            low = jnp.where(diagonal, table[j, 129:130, :].astype(F32), 0.0).astype(BF)
            left = jnp.concatenate([hot, high, low], axis=1)
            new = jnp.dot(left, right[...], preferred_element_type=F32)
            total = table[j, 0:128, :].astype(F32) + new[:, :128] + centroids[rows, :]
            result[rows, :] = total / (new[:, 128:] + 1.0)
        rows = pl.ds(512 * i, 512)
        copy = pltpu.make_async_copy(result.at[rows], updated.at[0, rows], save_sem.at[i])
        copy.start()
        saves.append(copy)
    save_own.wait()
    for copy in saves:
        copy.wait()


def on_device(
    tokens, lengths, w_up, up_bias, w_down, down_bias, ln_gain, ln_bias, stored, stored_codes, new_codes, centroids
):
    hbm = pl.BlockSpec(memory_space=pltpu.HBM)
    e_all, table = pl.pallas_call(
        layer_kernel,
        out_shape=(
            jax.ShapeDtypeStruct((NZ, NX, 32, 128), BF),
            jax.ShapeDtypeStruct((32, 144, 128), BF),
        ),
        in_specs=[hbm, hbm, hbm, hbm, hbm, hbm, hbm, hbm, hbm, hbm],
        out_specs=(hbm, hbm),
        scratch_shapes=[
            pltpu.SMEM((1, 1, 4), jnp.int32),
            pltpu.VMEM((1, 128), BF),
            pltpu.VMEM((1, 1024), F32),
            pltpu.VMEM((1, 1024), F32),
            pltpu.VMEM((1, 1024), F32),
            pltpu.VMEM((1, 2048), jnp.int32),
            pltpu.VMEM((4, 512, 1024), BF),
            pltpu.VMEM((2, 4, 4, 32, 1024), BF),
            pltpu.VMEM((2, 4, 4, 32, 1024), BF),
            pltpu.VMEM((4, 512, 1024), F32),
            pltpu.VMEM((3, 512, 1024), BF),
            pltpu.VMEM((3, 512, 1024), BF),
            pltpu.VMEM((2048, 256), BF),
            pltpu.VMEM((32, 144, 128), BF),
            pltpu.VMEM((2, 4, 144, 128), BF),
            pltpu.VMEM((2, 8, 144, 128), BF),
            pltpu.VMEM((7, 144, 128), BF),
            pltpu.VMEM((32, 144, 128), BF),
            pltpu.VMEM((4, 8, 8, 128), F32),
            pltpu.VMEM((8, 8, 128), F32),
            pltpu.VMEM((8, 8, 128), F32),
            pltpu.VMEM((NX, NZ, 32, 128), BF),
            pltpu.VMEM((8, 1024), F32),
            pltpu.SemaphoreType.DMA,
            pltpu.SemaphoreType.DMA((121,)),
            pltpu.SemaphoreType.DMA((16,)),
        ],
        compiler_params=pltpu.CompilerParams(
            collective_id=0, has_side_effects=True, vmem_limit_bytes=64 * 1024 * 1024
        ),
    )(
        tokens, w_up, w_down, stored, lengths, up_bias.reshape(1, 128), down_bias.reshape(1, 1024),
        ln_gain.reshape(1, 1024), ln_bias.reshape(1, 1024), stored_codes,
    )
    embeds, updated = pl.pallas_call(
        update_kernel,
        out_shape=(
            jax.ShapeDtypeStruct((32, 128), BF),
            jax.ShapeDtypeStruct((1, 4096, 128), F32),
        ),
        in_specs=[hbm, hbm, hbm, hbm],
        out_specs=(hbm, hbm),
        scratch_shapes=[
            pltpu.VMEM((1024, 128), BF),
            pltpu.VMEM((1, 1024), jnp.int32),
            pltpu.VMEM((32, 144, 128), BF),
            pltpu.VMEM((4096, 128), F32),
            pltpu.VMEM((4096, 128), F32),
            pltpu.VMEM((1280, 256), BF),
            pltpu.SemaphoreType.DMA((18,)),
            pltpu.SemaphoreType.DMA((8,)),
        ],
        compiler_params=pltpu.CompilerParams(vmem_limit_bytes=64 * 1024 * 1024),
    )(e_all.reshape(1024, 128), new_codes, table, centroids)
    return embeds, updated


def solution(mesh):
    return jax.shard_map(
        on_device,
        mesh=mesh,
        in_specs=(
            P(("dp", "sub"), None),
            P("dp", "sub", None),
            P("dp", None),
            P("dp"),
            P("dp", None),
            P(),
            P(),
            P(),
            P("dp", "sub"),
            P("sub", "dp"),
            P("sub", None),
            P("sub", None, None),
        ),
        out_specs=(P("dp", "sub"), P("sub", None, None)),
        check_vma=False,
    )
```

time: 441 us -> 92.5 us (0.21)
  waiting for transfers between devices: 199 us -> 0 us
  blocking collectives: 147 us -> 0 us
  Pallas kernels: 0 us -> 91.6 us
  matrix products: 45.1 us -> 0 us
  other arithmetic: 14 us -> 0 us
  between operations: 13.8 us -> 0.82 us
  local copies, waits for them, and re-layouts: 6.44 us -> 0 us
  loops' own time: 5.45 us -> 0 us
  starting transfers between devices: 5.43 us -> 0 us
    all_gather x2 -> x0, waiting for transfers between devices: 164 us -> none  [the longest x1 98 us: on_device(): down_rows = lax.all_gather(w_down, 'dp', axis=0, tiled=True)]
    psum x1 -> x0, blocking collectives: 112 us -> none  [on_device(): lax.psum(counts.astype(jnp.bfloat16), 'dp').astype(jnp.float32)]
    pallas_call x0 -> x2, Pallas kernels: none -> 91.6 us  [the longest x1 85.3 us: on_device(): pl.pallas_call(layer_kernel, out_shape=(jax.ShapeDtypeStruct((NZ, NX, 32,...]
    dot_general x10 -> x0, matrix products: 45.1 us -> none  [the longest x1 30.8 us: on_device(): ffn_total = jnp.dot(hidden, down_rows, preferred_element_type=jnp.float32)]
    all_gather x1 -> x0, blocking collectives: 35.5 us -> none  [on_device(): bias_matrix_rows = lax.all_gather(up_bias, 'dp', axis=0, tiled=True)]
    psum x1 -> x0, waiting for transfers between devices: 29.1 us -> none  [on_device(): lax.psum(centroid_totals.astype(jnp.bfloat16), 'dp').astype(jnp.float32)]
    reduce_sum x9 -> x0, other arithmetic: 8.12 us -> none  [the longest x8 7.77 us: one_group(): counts = jnp.sum(assignment_matrix, axis=2, dtype=jnp.float32)]
    another operation x1 -> x0, loops' own time: 5.45 us -> none  [code_tallies(): lax.map(one_group, jnp.arange(code_count // width_codes, dtype=jnp.int32))]
  transfers between devices with their start and end apart: 4 -> 0, of which waited for: 4 -> 0; matrix products, arithmetic and copies ran while one was open for 1% -> 0% of each run, Pallas kernels for 0% -> 0%
where the time goes in v2:
time: 92.5 us; the launch traced here: 92.4 us
  Pallas kernels  91.6 us (99%)
    pallas_call x1, Pallas kernels, on_device(): pl.pallas_call(layer_kernel, out_shape=(jax.ShapeDtypeStruct((NZ, NX, 32,...  85.3 us
    pallas_call x1, Pallas kernels, on_device(): pl.pallas_call(update_kernel, out_shape=(jax.ShapeDtypeStruct((32, 128),...  6.29 us

profile of v2, /device:TPU:1, one launch (start us, length us, event | category | flops | bytes accessed | tf_op | source)
XLA Modules:
  0.0 92.4 jit_solution(10243273653521951871)
XLA Ops:
  0.6 85.3 %shard_map.131 = (bf16[8,4,32,128]{3,2,1,0:T(8,128)(2,1)}, bf16[32,144,128]{2,1,0:T(8,128)(2,1)}) custom-call(bf16[512,1024]{1,0:T(8,128)(2,1)} %tokens.1, bf16[128,1024]{1,0:T(8,128)(2,1)} %w_up.1, bf16[128,1024]{1,0:T(8,128)(2,1)} %w_down.1, bf16[2048,128]{1,0:T(8,128)(2,1)} %stored.1, s32[1,1,4]{2,1,0:T(1,128)} %lengths_in.1, bf16[1,128]{1,0:T(2,128)(2,1)} %bitcast.9, ...), custom_call_target="tpu_custom_call" | custom-call | tf_op jit(solution)/shard_map/pallas_call | solution.py:431
  85.9 6.3 %shard_map.132 = (bf16[32,128]{1,0:T(8,128)(2,1)}, f32[1,4096,128]{2,1,0:T(8,128)}) custom-call(bf16[1024,128]{1,0:T(8,128)(2,1)} %bitcast.5, s32[1,1024]{1,0:T(1,128)} %codes_in.3, bf16[32,144,128]{2,1,0:T(8,128)(2,1)} %get-tuple-element.5.table_in, f32[1,4096,128]{2,1,0:T(8,128)} %centroids_in.1), custom_call_target="tpu_custom_call" | custom-call | tf_op jit(solution)/shard_map/pallas_call | solution.py:474

commit v3 on v2

--- a/solution.py
+++ b/solution.py
@@ -35,11 +35,10 @@
     242, 243, 324, 332, 334, 301, 321, 23, 213, 214, 103, 104, 300, 310, 113, 114, 316, 306, 203, 204, 311, 331,
     305, 325, 315, 335, 22, 272, 273, 262, 263, 21, 223, 224, 233, 234, 20, 321, 243, 244, 253, 254, 104, 214, 204,
     114, 307, 317, 325, 273, 274, 263, 264, 331, 27, 335, 224, 234, 244, 254, 26, 300, 320, 306, 326, 25, 274, 316,
-    336, 264, 310, 330, 24, 307, 327, 317, 337, 31, 375, 374, 10, 380, 29, 320, 326, 30, 336, 330, 327, 337, 28, 46,
-    364, 47, 365, 44, 45, 42, 366, 43, 367, 40, 41, 364, 51, 361, 50, 360, 380, 11, 381, 365, 52, 362, 53, 363, 366,
-    367, 381, 376, 377, 361, 360, 54, 55, 362, 363, 56, 57, 58, 382, 382, 59, 400, 393, 395, 392, 396, 394, 391,
-    397, 376, 378, 377, 379, 400, 391, 401, 397, 407, 392, 402, 396, 406, 393, 403, 395, 405, 394, 404, 401, 407,
-    402, 406, 403, 405, 404, 378, 379,
+    336, 264, 310, 330, 24, 307, 327, 317, 337, 31, 375, 374, 10, 380, 320, 326, 30, 336, 330, 327, 337, 46, 364,
+    47, 365, 44, 364, 50, 360, 51, 361, 45, 365, 52, 362, 53, 363, 29, 42, 366, 43, 367, 380, 11, 381, 28, 40, 41,
+    366, 367, 360, 54, 361, 55, 381, 376, 377, 362, 56, 363, 57, 58, 382, 382, 59, 393, 395, 392, 396, 394, 391,
+    397, 376, 378, 377, 379, 391, 397, 392, 396, 393, 395, 394, 400, 378, 379, 400,
 )
 
 
@@ -183,10 +182,9 @@
     copies[381] = [(ff.at[own + z], ff.at[own + z], z_peer(k)) for k in range(1, NZ)]
     copies[382] = [(em.at[(s + k) % NS], er.at[s], s_peer(k)) for k in range(1, NS)]
     for k in range(NZ):
-        row = (z - k + NZ) % NZ
         if k:
             copies[390 + k] = [(ee.at[x, z], ee.at[x, z], z_peer(k))]
-        copies[400 + k] = [(ee.at[x, row], ee.at[x, row], x_peer(j)) for j in (2, 1, 3)]
+    copies[400] = [(ee.at[x], ee.at[x], x_peer(j)) for j in (2, 1, 3)]
 
     compute = {}
 
@@ -345,7 +343,7 @@
             if len(copies[name]) > 1:
                 whole = landing.get(name)
                 if whole is None:
-                    whole = ee.at[0, pl.ds(0, 3)]
+                    whole = ee.at[pl.ds(0, 3)]
                 copy = remote(whole, whole, device, arrival)
             running[name] = copy
         else:

time: 92.5 us -> 89.5 us (0.968)
  Pallas kernels: 91.6 us -> 88.6 us
    pallas_call x1, Pallas kernels: 85.3 us -> 82.3 us  [on_device(): pl.pallas_call(layer_kernel, out_shape=(jax.ShapeDtypeStruct((NZ, NX, 32,...]
where the time goes in v3:
time: 89.5 us; the launch traced here: 89.4 us
  Pallas kernels  88.6 us (99%)
    pallas_call x1, Pallas kernels, on_device(): pl.pallas_call(layer_kernel, out_shape=(jax.ShapeDtypeStruct((NZ, NX, 32,...  82.3 us
    pallas_call x1, Pallas kernels, on_device(): pl.pallas_call(update_kernel, out_shape=(jax.ShapeDtypeStruct((32, 128),...  6.31 us

profile of v3, /device:TPU:1, one launch (start us, length us, event | category | flops | bytes accessed | tf_op | source)
XLA Modules:
  0.0 89.4 jit_solution(8018998849254488182)
XLA Ops:
  0.6 82.3 %shard_map.131 = (bf16[8,4,32,128]{3,2,1,0:T(8,128)(2,1)}, bf16[32,144,128]{2,1,0:T(8,128)(2,1)}) custom-call(bf16[512,1024]{1,0:T(8,128)(2,1)} %tokens.1, bf16[128,1024]{1,0:T(8,128)(2,1)} %w_up.1, bf16[128,1024]{1,0:T(8,128)(2,1)} %w_down.1, bf16[2048,128]{1,0:T(8,128)(2,1)} %stored.1, s32[1,1,4]{2,1,0:T(1,128)} %lengths_in.1, bf16[1,128]{1,0:T(2,128)(2,1)} %bitcast.9, ...), custom_call_target="tpu_custom_call" | custom-call | tf_op jit(solution)/shard_map/pallas_call | solution.py:429
  82.9 6.3 %shard_map.132 = (bf16[32,128]{1,0:T(8,128)(2,1)}, f32[1,4096,128]{2,1,0:T(8,128)}) custom-call(bf16[1024,128]{1,0:T(8,128)(2,1)} %bitcast.5, s32[1,1024]{1,0:T(1,128)} %codes_in.3, bf16[32,144,128]{2,1,0:T(8,128)(2,1)} %get-tuple-element.5.table_in, f32[1,4096,128]{2,1,0:T(8,128)} %centroids_in.1), custom_call_target="tpu_custom_call" | custom-call | tf_op jit(solution)/shard_map/pallas_call | solution.py:472

commit v4 on v3

--- a/solution.py
+++ b/solution.py
@@ -27,18 +27,18 @@
 
 
 ORDER = (
-    101, 111, 340, 341, 354, 370, 201, 211, 352, 353, 355, 350, 313, 303, 0, 1, 2, 3, 4, 340, 342, 221, 231, 341,
-    343, 241, 251, 370, 371, 350, 5, 101, 102, 302, 312, 111, 112, 304, 314, 201, 202, 211, 212, 313, 333, 303, 323,
-    6, 7, 373, 372, 342, 343, 261, 271, 231, 232, 221, 222, 251, 252, 241, 242, 333, 323, 371, 354, 358, 302, 322,
-    102, 103, 301, 311, 112, 113, 305, 315, 202, 203, 212, 213, 352, 356, 353, 357, 355, 359, 312, 332, 304, 324,
-    314, 334, 358, 261, 262, 271, 272, 372, 373, 9, 375, 8, 374, 356, 357, 359, 222, 223, 232, 233, 322, 252, 253,
-    242, 243, 324, 332, 334, 301, 321, 23, 213, 214, 103, 104, 300, 310, 113, 114, 316, 306, 203, 204, 311, 331,
-    305, 325, 315, 335, 22, 272, 273, 262, 263, 21, 223, 224, 233, 234, 20, 321, 243, 244, 253, 254, 104, 214, 204,
-    114, 307, 317, 325, 273, 274, 263, 264, 331, 27, 335, 224, 234, 244, 254, 26, 300, 320, 306, 326, 25, 274, 316,
-    336, 264, 310, 330, 24, 307, 327, 317, 337, 31, 375, 374, 10, 380, 320, 326, 30, 336, 330, 327, 337, 46, 364,
-    47, 365, 44, 364, 50, 360, 51, 361, 45, 365, 52, 362, 53, 363, 29, 42, 366, 43, 367, 380, 11, 381, 28, 40, 41,
-    366, 367, 360, 54, 361, 55, 381, 376, 377, 362, 56, 363, 57, 58, 382, 382, 59, 393, 395, 392, 396, 394, 391,
-    397, 376, 378, 377, 379, 391, 397, 392, 396, 393, 395, 394, 400, 378, 379, 400,
+    350, 340, 354, 111, 370, 353, 303, 341, 201, 0, 313, 1, 101, 211, 2, 3, 4, 352, 341, 241, 111, 340, 370, 251,
+    350, 343, 342, 5, 304, 371, 221, 6, 313, 112, 211, 101, 303, 312, 7, 355, 323, 372, 373, 102, 314, 201, 231,
+    202, 221, 222, 343, 212, 231, 241, 352, 232, 353, 302, 242, 251, 357, 342, 112, 212, 113, 315, 102, 261, 311,
+    301, 222, 314, 355, 334, 323, 304, 354, 271, 305, 103, 333, 302, 252, 322, 202, 232, 373, 203, 324, 372, 8, 213,
+    358, 261, 9, 375, 223, 301, 374, 356, 371, 262, 20, 233, 312, 321, 103, 271, 310, 311, 113, 242, 331, 358, 272,
+    356, 252, 306, 324, 357, 322, 243, 333, 359, 332, 359, 253, 104, 305, 22, 262, 223, 114, 263, 203, 21, 213, 272,
+    233, 273, 332, 23, 331, 321, 224, 315, 234, 300, 214, 243, 104, 114, 253, 334, 316, 204, 244, 254, 310, 263,
+    317, 26, 325, 307, 27, 375, 264, 273, 274, 374, 10, 335, 380, 25, 234, 300, 306, 204, 330, 326, 316, 307, 320,
+    336, 327, 317, 214, 337, 224, 31, 24, 264, 330, 274, 30, 29, 325, 326, 320, 336, 327, 244, 254, 337, 335, 46,
+    364, 44, 47, 364, 50, 360, 380, 365, 11, 381, 42, 28, 365, 45, 52, 51, 362, 40, 366, 53, 43, 361, 366, 367, 367,
+    363, 41, 381, 376, 377, 360, 362, 54, 361, 55, 56, 363, 57, 58, 382, 382, 59, 397, 392, 393, 395, 391, 394, 376,
+    377, 378, 379, 396, 392, 394, 391, 396, 393, 397, 395, 400, 379, 378, 60, 400,
 )
 
 
@@ -323,6 +323,8 @@
 
     compute[58] = embed
     compute[59] = own_rows
+    saves = []
+    compute[60] = lambda: saves.append(local(ff, f_out))
 
     landing = {
         370: bb.at[0, pl.ds(1, 7)], 371: bb.at[pl.ds(1, 3)], 380: rc, 381: rc, 382: er.at[pl.ds(1, 7)],
@@ -348,7 +350,7 @@
             running[name] = copy
         else:
             compute[name]()
-    saves = [local(ff, f_out)] + [local(ee.at[i], e_out.at[:, i]) for i in range(NX)]
+    saves += [local(ee.at[i], e_out.at[:, i]) for i in range(NX)]
     total = 0
     for ends in copies.values():
         for source, _, _ in ends:

time: 89.5 us -> 87.7 us (0.980)
  Pallas kernels: 88.6 us -> 86.8 us
    pallas_call x1, Pallas kernels: 82.3 us -> 80.5 us  [on_device(): pl.pallas_call(layer_kernel, out_shape=(jax.ShapeDtypeStruct((NZ, NX, 32,...]
where the time goes in v4:
time: 87.7 us; the launch traced here: 87.6 us
  Pallas kernels  86.8 us (99%)
    pallas_call x1, Pallas kernels, on_device(): pl.pallas_call(layer_kernel, out_shape=(jax.ShapeDtypeStruct((NZ, NX, 32,...  80.5 us
    pallas_call x1, Pallas kernels, on_device(): pl.pallas_call(update_kernel, out_shape=(jax.ShapeDtypeStruct((32, 128),...  6.3 us

profile of v4, /device:TPU:1, one launch (start us, length us, event | category | flops | bytes accessed | tf_op | source)
XLA Modules:
  0.0 87.6 jit_solution(15278906868678470677)
XLA Ops:
  0.6 80.5 %shard_map.131 = (bf16[8,4,32,128]{3,2,1,0:T(8,128)(2,1)}, bf16[32,144,128]{2,1,0:T(8,128)(2,1)}) custom-call(bf16[512,1024]{1,0:T(8,128)(2,1)} %tokens.1, bf16[128,1024]{1,0:T(8,128)(2,1)} %w_up.1, bf16[128,1024]{1,0:T(8,128)(2,1)} %w_down.1, bf16[2048,128]{1,0:T(8,128)(2,1)} %stored.1, s32[1,1,4]{2,1,0:T(1,128)} %lengths_in.1, bf16[1,128]{1,0:T(2,128)(2,1)} %bitcast.9, ...), custom_call_target="tpu_custom_call" | custom-call | tf_op jit(solution)/shard_map/pallas_call | solution.py:431
  81.1 6.3 %shard_map.132 = (bf16[32,128]{1,0:T(8,128)(2,1)}, f32[1,4096,128]{2,1,0:T(8,128)}) custom-call(bf16[1024,128]{1,0:T(8,128)(2,1)} %bitcast.5, s32[1,1024]{1,0:T(1,128)} %codes_in.3, bf16[32,144,128]{2,1,0:T(8,128)(2,1)} %get-tuple-element.5.table_in, f32[1,4096,128]{2,1,0:T(8,128)} %centroids_in.1), custom_call_target="tpu_custom_call" | custom-call | tf_op jit(solution)/shard_map/pallas_call | solution.py:474
